TPU v7x, 32 devices: a whole 2x2x4 slice. The times are simulated.
32 devices in a mesh: dp: 16 (over z, y, core), mp: 2 (over x).
Axes of the slice: x: 2, y: 2, z: 4, core: 2. Of those that a mesh axis runs over, the one named last changes fastest.
Arguments:
- activations: bfloat16 [16384, 4096], P('dp', 'mp'), may hold values from -6 to 6
- out_grad: bfloat16 [16384, 14336], P('dp', 'mp'), may hold values from -0.046875 to 0.046875
- tile_list: int32 [2, 16, 2], P('mp'), may hold values from 0 to 111, as said below
- tile_count: int32 [2], P('mp'), may hold values from 8 to 16, as said below
Outputs:
- grad_tiles: float32 [2, 16, 128, 128], P('mp', 'dp')
Inputs may be any that keep to these rules, and one draw needn't show every extreme that they name: `tile_list`: in shard c the 16 entries name distinct blocks; the block row lies in 0 to 31 and the block column in c * 56 to (c + 1) * 56 - 1. `tile_count`: some shard has all 16 slots live.
All inputs are finite; a program needn't handle non-finite values.
Results may differ from a plain program's by a relative error of at most 0.0003.
Values may be sent and summed in bfloat16 or wider, within the bound.
No kernel may reach another device: no remote copies, remote signals or barrier semaphores. Data moves between devices by JAX's collectives and lax.ppermute only.
A program may use at most 128 MiB of HBM per device.

v0:
```python
import math

import jax
import jax.numpy as jnp
from jax import lax
from jax.sharding import PartitionSpec as P

D = 4096
BLK = 128


def on_device(activations, out_grad, tile_list, tile_count):
    gathered = lax.all_gather(activations, "mp", axis=1, tiled=True)
    token_count = gathered.shape[0]
    slot_total = tile_list.shape[1]
    col_blocks = out_grad.shape[1] // BLK
    row_ids = tile_list[0, :, 0]
    col_ids = tile_list[0, :, 1] - lax.axis_index("mp") * col_blocks
    active = (jnp.arange(slot_total, dtype=jnp.int32) < tile_count[0]).astype(jnp.float32)
    act_blocks = gathered.reshape(token_count, D // BLK, BLK)
    grad_blocks = out_grad.reshape(token_count, col_blocks, BLK)

    def group_product(indices):
        act_sel = jnp.take(act_blocks, indices[0], axis=1)
        grad_sel = jnp.take(grad_blocks, indices[1], axis=1)
        return jnp.einsum("tkr,tkc->krc", act_sel, grad_sel, preferred_element_type=jnp.float32)

    count = row_ids.shape[0]
    group_size = math.gcd(count, 16)
    result = lax.map(
        group_product, (row_ids.reshape(-1, group_size), col_ids.reshape(-1, group_size))
    )
    summed = lax.psum_scatter(
        result.reshape(count, BLK, BLK) * active[:, None, None],
        "dp",
        scatter_dimension=0,
        tiled=True,
    )
    return summed[None]


def solution(mesh):
    placed = (P("dp", "mp"), P("dp", "mp"), P("mp", None, None), P("mp"))
    return jax.shard_map(
        on_device, mesh=mesh, in_specs=placed, out_specs=P("mp", "dp", None, None), check_vma=False
    )
```

profile of v0, /device:TPU:0, one launch (start us, length us, event | category | flops | bytes accessed | tf_op | source)
XLA Modules:
  0.0 208.7 jit_solution(6277323262940259520)
XLA Ops:
  6.5 0.0 all-gather.2.cloned.1.call-start
  6.5 6.4 %copy.7 = bf16[1024,2048]{0,1:T(8,128)(2,1)} copy(bf16[1024,2048]{1,0:T(8,128)(2,1)} %param.4) | data formatting | bytes 8388608 | tf_op args[0]
  12.9 0.0 all-gather.2.cloned.1.call-update
  13.0 0.0 reduce-scatter.2.cloned.1.call-start
  13.0 20.4 %copy.9 = bf16[1024,7168]{0,1:T(8,128)(2,1)} copy(bf16[1024,7168]{1,0:T(8,128)(2,1)} %param.5) | data formatting | bytes 29360128 | tf_op args[1]
  33.4 0.0 copy-start
  33.4 19.9 %copy.10 = bf16[1024,56,128]{2,0,1:T(8,128)(2,1)} copy(bf16[1024,56,128]{0,2,1:T(8,128)(2,1)} %bitcast.27) | data formatting | bytes 29360128 | tf_op jit(solution)/shard_map/reshape | solution.py:21
  53.9 0.0 copy-done
  53.9 8.2 %gather_fusion.1 = bf16[16,1024,128]{2,1,0:T(8,128)(2,1)} fusion(bf16[1024,56,128]{2,0,1:T(8,128)(2,1)} %copy.10, s32[1024]{0:T(1024)S(1)} %get-tuple-element.26), kind=kCustom, calls=%fused_computation.1 | custom fusion | bytes 8388672 | tf_op jit(solution)/shard_map/while/body/eval_jaxpr/jit(_take)/gather | solution.py:25
  62.2 57.6 %all-gather.2.cloned.1.call-done = bf16[1024,4096]{0,1:T(8,128)(2,1)} async-done(((bf16[1024,2048]{0,1:T(8,128)(2,1)}), bf16[1024,4096]{0,1:T(8,128)(2,1)}) %all-gather.2.cloned.1.call-update) | async-done | bytes 8388624 | tf_op jit(solution)/shard_map/all_gather | solution.py:13
  119.8 11.9 %copy.8 = bf16[1024,32,128]{2,0,1:T(8,128)(2,1)} copy(bf16[1024,32,128]{0,2,1:T(8,128)(2,1)} %bitcast.28) | data formatting | bytes 16777216 | tf_op jit(solution)/shard_map/reshape | solution.py:20
  131.8 6.4 %gather_fusion = bf16[16,1024,128]{2,1,0:T(8,128)(2,1)} fusion(bf16[1024,32,128]{2,0,1:T(8,128)(2,1)} %copy.8, s32[1024]{0:T(1024)S(1)} %get-tuple-element.28), kind=kCustom, calls=%fused_computation | custom fusion | bytes 8388672 | tf_op jit(solution)/shard_map/while/body/eval_jaxpr/jit(_take)/gather | solution.py:24
  138.2 6.2 %fusion.8 = f32[16,128,128]{2,1,0:T(8,128)} fusion(bf16[16,1024,128]{2,1,0:T(8,128)(2,1)} %gather_fusion.1, pred[16]{0:T(512)(128)(4,1)S(1)} %get-tuple-element.16, bf16[16,1024,128]{2,1,0:T(8,128)(2,1)} %gather_fusion, pred[16]{0:T(512)(128)(4,1)S(1)} %get-tuple-element.15, f32[16]{0:T(128)S(1)} %compare_convert_fusion), kind=kOutput, calls=%fused_computation.10 | convolution fusion | flops 541327360 | bytes 9437280 | tf_op jit(solution)/shard_map/while/body/eval_jaxpr/tkr,tkc->krc/dot_general | solution.py:26
  144.3 0.0 reduce-scatter.2.cloned.1.call-update
  144.4 57.5 %reduce-scatter.2.cloned.1.call-done = f32[1,128,128]{2,1,0:T(8,128)} async-done(((f32[16,128,128]{2,1,0:T(8,128)}), f32[1,128,128]{2,1,0:T(8,128)}) %reduce-scatter.2.cloned.1.call-update) | async-done | bytes 65552 | tf_op jit(solution)/shard_map/reduce_scatter | solution.py:33
  (4 shorter events, 0.0 us)
Async XLA Ops:
  6.5 113.3 %all-gather.2.cloned.1.call-start = ((), (), s32[]{:S(2)}) async-start(), calls=%async_computation.1 | async-start | bytes 12582912 | tf_op jit(solution)/shard_map/all_gather | solution.py:13
  13.0 188.9 %reduce-scatter.2.cloned.1.call-start = ((), (), s32[]{:S(2)}) async-start(), calls=%async_computation.2 | async-start | bytes 1114112 | tf_op jit(solution)/shard_map/reduce_scatter | solution.py:33
  33.4 20.5 %copy-start = (s32[1,16,2]{1,2,0:T(2,128)S(1)}, s32[1,16,2]{1,2,0:T(2,128)}, u32[]{:S(2)}) copy-start(s32[1,16,2]{1,2,0:T(2,128)} %param.6) | copy-start | bytes 388
Sparse Core Ops, SparseCore 0:
  13.1 106.6 all-gather.1
  144.5 57.3 reduce-scatter.1
where the time goes:
time: 210 us; the launch traced here: 209 us
  waiting for transfers between devices  115 us (55%)
  local copies, waits for them, and re-layouts  73.2 us (35%)
  between operations  14.1 us (7%)
  matrix products  6.15 us (3%)
    all_gather x1, waiting for transfers between devices, on_device(): gathered = lax.all_gather(activations, 'mp', axis=1, tiled=True)  57.6 us
    reduce_scatter x1, waiting for transfers between devices, on_device(): lax.psum_scatter(result.reshape(count, BLK, BLK) * active[:, None, None],...  57.5 us
    unnamed x4, local copies, waits for them, and re-layouts  26.7 us
    reshape x1, local copies, waits for them, and re-layouts, on_device(): grad_blocks = out_grad.reshape(token_count, col_blocks, BLK)  19.9 us
    reshape x1, local copies, waits for them, and re-layouts, on_device(): act_blocks = gathered.reshape(token_count, D // BLK, BLK)  11.9 us
    gather x1, local copies, waits for them, and re-layouts, group_product(): grad_sel = jnp.take(grad_blocks, indices[1], axis=1)  8.23 us
    gather x1, local copies, waits for them, and re-layouts, group_product(): act_sel = jnp.take(act_blocks, indices[0], axis=1)  6.43 us
    dot_general x1, matrix products, group_product(): jnp.einsum('tkr,tkc->krc', act_sel, grad_sel, preferred_element_type=jnp....  6.15 us
  transfers between devices with their start and end apart: 2, of which 2 were waited for; matrix products, arithmetic and copies ran while one was open for 23% of the time, Pallas kernels for 0%

commit v1 on v0

v1 whole, which is shorter than its diff:
```python
import functools

import jax
import jax.numpy as jnp
from jax import lax
from jax.experimental import pallas as pl
from jax.experimental.pallas import tpu as pltpu
from jax.sharding import PartitionSpec as P

BLK = 128
VMEM_BYTES = 40 * 1024 * 1024
SCALARS = pl.BlockSpec(memory_space=pltpu.SMEM)
ANYWHERE = pl.BlockSpec(memory_space=pl.ANY)
IN_VMEM = pl.BlockSpec(memory_space=pltpu.VMEM)


def plan_kernel(shards, row_blocks, *refs):
    lists, (most_ref, send_ref, place_ref, seen) = refs[:shards], refs[shards:]
    slots = (lists[0].shape[0] - 1) // 2
    me = lax.axis_index("mp")

    def scan(list_ref, origin, note_slot, note_block):
        for b in range(row_blocks):
            seen[b] = -1

        def step(k, count):
            block = list_ref[2 * k] - origin * row_blocks
            wanted = (k < list_ref[2 * slots]) & (block >= 0) & (block < row_blocks)
            at = jnp.clip(block, 0, row_blocks - 1)
            new = wanted & (seen[at] < 0)

            @pl.when(new)
            def _():
                seen[at] = count
                note_block(count, at)

            note_slot(k, jnp.where(wanted, seen[at], -1))
            return count + new.astype(jnp.int32)

        return lax.fori_loop(0, slots, step, jnp.int32(0))

    def skip(*_):
        pass

    for shift in range(1, shards):
        for b in range(row_blocks):
            send_ref[(shift - 1) * row_blocks + b] = 0

        def note_block(count, block):
            send_ref[(shift - 1) * row_blocks + count] = block

        def note_slot(k, place):
            place_ref[(shift - 1) * slots + k] = place

        most = jnp.int32(0)
        for s in range(shards):
            origin = lax.rem(me - s - shift + 2 * shards, shards)
            count = scan(
                lists[s],
                origin,
                note_slot if s == 0 else skip,
                note_block if s == shards - shift else skip,
            )
            most = jnp.maximum(most, count)
        most_ref[shift - 1] = most


def make_plan(shards, row_blocks, lists):
    slots = (lists[0].shape[0] - 1) // 2
    return pl.pallas_call(
        functools.partial(plan_kernel, shards, row_blocks),
        out_shape=(
            jax.ShapeDtypeStruct((shards - 1,), jnp.int32),
            jax.ShapeDtypeStruct(((shards - 1) * row_blocks,), jnp.int32),
            jax.ShapeDtypeStruct(((shards - 1) * slots,), jnp.int32),
        ),
        in_specs=[SCALARS] * shards,
        out_specs=(SCALARS,) * 3,
        scratch_shapes=[pltpu.SMEM((row_blocks,), jnp.int32)],
        name="plan",
    )(*lists)


def pack_kernel(shift, row_blocks, send_ref, act_ref, out_ref, sems):
    def copy(j):
        block = send_ref[(shift - 1) * row_blocks + j]
        source = act_ref.at[:, pl.ds(pl.multiple_of(block * BLK, BLK), BLK)]
        return pltpu.make_async_copy(source, out_ref.at[j], sems.at[j])

    @pl.loop(0, out_ref.shape[0])
    def _(j):
        copy(j).start()

    @pl.loop(0, out_ref.shape[0])
    def _(j):
        copy(j).wait()


def pack(shift, row_blocks, send, activations, count):
    tokens = activations.shape[0]
    return pl.pallas_call(
        functools.partial(pack_kernel, shift, row_blocks),
        out_shape=jax.ShapeDtypeStruct((count, tokens, BLK), activations.dtype),
        in_specs=[SCALARS, ANYWHERE],
        out_specs=IN_VMEM,
        scratch_shapes=[pltpu.SemaphoreType.DMA((count,))],
        cost_estimate=pl.CostEstimate(
            flops=0, bytes_accessed=count * tokens * BLK * 4, transcendentals=0
        ),
        name="pack",
    )(send, activations)


def tiles_kernel(owners, row_blocks, shift, list_ref, place_ref, rows_ref, grad_ref, *rest):
    if shift:
        rest = rest[2:]
    keep_ref, send_ref, row_buf, grad_buf, stage, row_sems, grad_sems, out_sems = rest
    slots = (list_ref.shape[0] - 1) // 2
    half = slots // 2
    lanes = slots // owners
    steps = owners.bit_length() - 1
    depth = row_buf.shape[0]
    me = lax.axis_index("dp")
    shard = lax.axis_index("mp")
    col_blocks = grad_ref.shape[1] // BLK

    def slot_of(place):
        owner = place // lanes
        relative = jnp.int32(0)
        for i in range(steps):
            relative = relative | (((owner >> (steps - 1 - i)) & 1) << i)
        return (me ^ relative) * lanes + place % lanes

    def block_of(slot):
        if shift:
            return place_ref[(shift - 1) * slots + slot]
        block = list_ref[2 * slot] - shard * row_blocks
        here = (block >= 0) & (block < row_blocks) & (slot < list_ref[2 * slots])
        return jnp.where(here, block, -1)

    def loads(place):
        slot = slot_of(place)
        block = block_of(slot)
        at = lax.rem(place, depth)
        first = jnp.maximum(block, 0)
        if shift:
            source = rows_ref.at[first]
        else:
            source = rows_ref.at[:, pl.ds(pl.multiple_of(first * BLK, BLK), BLK)]
        column = list_ref[2 * slot + 1] - shard * col_blocks
        return (
            block >= 0,
            pltpu.make_async_copy(source, row_buf.at[at], row_sems.at[at]),
            pltpu.make_async_copy(
                grad_ref.at[:, pl.ds(pl.multiple_of(column * BLK, BLK), BLK)],
                grad_buf.at[at],
                grad_sems.at[at],
            ),
        )

    def start(place):
        used, row_copy, grad_copy = loads(place)

        @pl.when(used)
        def _():
            row_copy.start()
            grad_copy.start()

    def out_copy(place, act):
        @pl.when(place < half)
        def _():
            act(pltpu.make_async_copy(stage.at[place], keep_ref.at[place], out_sems.at[place]))

        @pl.when(place >= half)
        def _():
            act(
                pltpu.make_async_copy(stage.at[place], send_ref.at[place - half], out_sems.at[place])
            )

    @pl.loop(0, depth)
    def _(place):
        start(place)

    @pl.loop(0, slots)
    def _(place):
        used, row_copy, grad_copy = loads(place)
        at = lax.rem(place, depth)

        @pl.when(used)
        def _():
            row_copy.wait()
            grad_copy.wait()
            stage[place] = lax.dot_general(
                row_buf[at],
                grad_buf[at],
                (((0,), (0,)), ((), ())),
                preferred_element_type=jnp.float32,
            )

        if not shift:

            @pl.when(jnp.logical_not(used))
            def _():
                stage[place] = jnp.zeros((BLK, BLK), jnp.float32)

            out_copy(place, lambda copy: copy.start())
        else:

            @pl.when(used)
            def _():
                out_copy(place, lambda copy: copy.start())

        if depth < slots:
            pl.when(place + depth < slots)(lambda: start(place + depth))

    @pl.loop(0, slots)
    def _(place):
        if shift:

            @pl.when(block_of(slot_of(place)) >= 0)
            def _():
                out_copy(place, lambda copy: copy.wait())
        else:
            out_copy(place, lambda copy: copy.wait())


def tiles(owners, row_blocks, shift, slot_list, places, rows, out_grad, partial=()):
    tokens = out_grad.shape[0]
    slots = (slot_list.shape[0] - 1) // 2
    depth = min(slots, 16)
    half = jax.ShapeDtypeStruct((slots // 2, BLK, BLK), jnp.float32)
    return pl.pallas_call(
        functools.partial(tiles_kernel, owners, row_blocks, shift),
        out_shape=(half, half),
        in_specs=[SCALARS, SCALARS, ANYWHERE, ANYWHERE] + [ANYWHERE] * len(partial),
        out_specs=(ANYWHERE,) * 2,
        scratch_shapes=[
            pltpu.VMEM((depth, tokens, BLK), rows.dtype),
            pltpu.VMEM((depth, tokens, BLK), out_grad.dtype),
            pltpu.VMEM((slots, BLK, BLK), jnp.float32),
            pltpu.SemaphoreType.DMA((depth,)),
            pltpu.SemaphoreType.DMA((depth,)),
            pltpu.SemaphoreType.DMA((slots,)),
        ],
        input_output_aliases={4: 0, 5: 1} if partial else {},
        compiler_params=pltpu.CompilerParams(vmem_limit_bytes=VMEM_BYTES),
        cost_estimate=pl.CostEstimate(
            flops=slots * tokens * BLK * BLK,
            bytes_accessed=slots * tokens * BLK * 2,
            transcendentals=0,
        ),
        name="tiles_moved" if shift else "tiles_here",
    )(slot_list, places, rows, out_grad, *partial)


def on_device(shards, owners, activations, out_grad, tile_list, tile_count):
    slots = tile_list.shape[1]
    row_blocks = activations.shape[1] // BLK

    slot_list = jnp.concatenate([tile_list.reshape(-1), tile_count])
    routes = [[(i, (i + s) % shards) for i in range(shards)] for s in range(shards)]
    lists = [slot_list] + [lax.ppermute(slot_list, "mp", routes[s]) for s in range(1, shards)]
    partial = tiles(owners, row_blocks, 0, slot_list, slot_list, activations, out_grad)
    most, send, places = make_plan(shards, row_blocks, lists)

    for shift in range(1, shards):

        def move(count, send, slot_list, places, partial, activations, out_grad):
            if count == 0:
                return partial
            packed = pack(shift, row_blocks, send, activations, count)
            arrived = lax.ppermute(packed, "mp", routes[shift])
            return tiles(owners, row_blocks, shift, slot_list, places, arrived, out_grad, partial)

        branches = [functools.partial(move, count) for count in range(min(row_blocks, slots) + 1)]
        partial = lax.switch(
            most[shift - 1], branches, send, slot_list, places, partial, activations, out_grad
        )

    keep, send = partial
    steps = owners.bit_length() - 1
    for i in range(steps):
        arrived = lax.ppermute(send, "dp", [(d, d ^ (1 << i)) for d in range(owners)])
        if i + 1 < steps:
            middle = keep.shape[0] // 2
            keep, send = keep[:middle] + arrived[:middle], keep[middle:] + arrived[middle:]
        else:
            keep = keep + arrived
    return keep[None]


def solution(mesh):
    placed = (P("dp", "mp"), P("dp", "mp"), P("mp", None, None), P("mp"))
    return jax.shard_map(
        functools.partial(on_device, mesh.shape["mp"], mesh.shape["dp"]),
        mesh=mesh,
        in_specs=placed,
        out_specs=P("mp", "dp", None, None),
        check_vma=False,
    )
```

time: 210 us -> 79.1 us (0.38)
  local copies, waits for them, and re-layouts: 73.2 us -> 1.35 us
  waiting for transfers between devices: 115 us -> 48.8 us
  Pallas kernels: 0 us -> 14 us
  between operations: 14.1 us -> 1.39 us
  starting transfers between devices: 0.04 us -> 11.2 us
  matrix products: 6.15 us -> 0 us
    all_gather x1 -> x0, waiting for transfers between devices: 57.6 us -> none  [on_device(): gathered = lax.all_gather(activations, 'mp', axis=1, tiled=True)]
    reduce_scatter x1 -> x0, waiting for transfers between devices: 57.5 us -> none  [on_device(): lax.psum_scatter(result.reshape(count, BLK, BLK) * active[:, None, None],...]
    ppermute x0 -> x6, waiting for transfers between devices: none -> 48.8 us  [the longest x1 34.7 us: move(): arrived = lax.ppermute(packed, 'mp', routes[shift])]
    reshape x2 -> x1, local copies, waits for them, and re-layouts: 31.8 us -> 0.09 us  [on_device(): slot_list = jnp.concatenate([tile_list.reshape(-1), tile_count])]
    unnamed x4 -> x3, local copies, waits for them, and re-layouts: 26.7 us -> 1.26 us
    gather x2 -> x0, local copies, waits for them, and re-layouts: 14.7 us -> none  [the longest x1 8.23 us: group_product(): grad_sel = jnp.take(grad_blocks, indices[1], axis=1)]
    pallas_call x0 -> x4, Pallas kernels: none -> 14 us  [the longest x2 9.01 us: tiles(): pl.pallas_call(functools.partial(tiles_kernel, owners, row_blocks, shift)...]
    ppermute x0 -> x6, starting transfers between devices: none -> 11.2 us  [the longest x4 6.54 us: on_device(): arrived = lax.ppermute(send, 'dp', [(d, d ^ 1 << i) for d in range(owners)])]
  transfers between devices with their start and end apart: 2 -> 6, of which waited for: 2 -> 5; matrix products, arithmetic and copies ran while one was open for 23% -> 0% of each run, Pallas kernels for 0% -> 6%
where the time goes in v1:
time: 79.1 us; the launch traced here: 77.7 us
  waiting for transfers between devices  48.8 us (62%)
  Pallas kernels  14 us (18%)
  starting transfers between devices  11.2 us (14%)
  between operations  1.39 us (2%)
  local copies, waits for them, and re-layouts  1.35 us (2%)
  other arithmetic  0.84 us (1%)
    ppermute x1, waiting for transfers between devices, move(): arrived = lax.ppermute(packed, 'mp', routes[shift])  34.7 us
    ppermute x4, waiting for transfers between devices, on_device(): arrived = lax.ppermute(send, 'dp', [(d, d ^ 1 << i) for d in range(owners)])  14.1 us
    pallas_call x2, Pallas kernels, tiles(): pl.pallas_call(functools.partial(tiles_kernel, owners, row_blocks, shift)...  9.01 us
    ppermute x4, starting transfers between devices, on_device(): arrived = lax.ppermute(send, 'dp', [(d, d ^ 1 << i) for d in range(owners)])  6.54 us
    pallas_call x1, Pallas kernels, pack(): pl.pallas_call(functools.partial(pack_kernel, shift, row_blocks), out_sha...  3.17 us
    ppermute x1, starting transfers between devices, on_device(): lax.ppermute(slot_list, 'mp', routes[s])  2.94 us
    pallas_call x1, Pallas kernels, make_plan(): pl.pallas_call(functools.partial(plan_kernel, shards, row_blocks), out_sh...  1.78 us
    ppermute x1, starting transfers between devices, move(): arrived = lax.ppermute(packed, 'mp', routes[shift])  1.75 us
  transfers between devices with their start and end apart: 6, of which 5 were waited for; matrix products, arithmetic and copies ran while one was open for 0% of the time, Pallas kernels for 6%

profile of v1, /device:TPU:0, one launch (start us, length us, event | category | flops | bytes accessed | tf_op | source)
XLA Modules:
  0.0 77.7 jit_solution(16982701433267105232)
XLA Ops:
  0.7 0.8 copy.38
  1.4 0.1 reshape.6
  1.5 0.1 pad_add_fusion.refs_0_.list_ref.place_ref
  1.6 2.9 %collective-permute-start.16 = (s32[33]{0:T(128)S(1)}, s32[33]{0:T(128)S(1)}, u32[]{:S(2)}, u32[]{:S(2)}) collective-permute-start(s32[33]{0:T(128)S(1)} %pad_add_fusion.refs_0_.list_ref.place_ref), channel_id=1, source_target_pairs={{0,1},{1,0},{2,3},{3,2},{4,5},{5,4},{6,7},{7,6},{8,9},{9,8},{10,11... | collective-permute-start | bytes 404 | tf_op jit(solution)/shard_map/ppermute | solution.py:262
  4.5 4.4 %tiles_here.1 = (f32[8,128,128]{2,1,0:T(8,128)S(1)}, f32[8,128,128]{2,1,0:T(8,128)S(1)}) custom-call(s32[33]{0:T(128)S(1)} %pad_add_fusion.refs_0_.list_ref.place_ref, s32[33]{0:T(128)S(1)} %pad_add_fusion.refs_0_.list_ref.place_ref, bf16[1024,2048]{1,0:T(8,128)(2,1)} %rows_ref.1, bf16[1024,7168]{1,0:T(8,128)(2,1)} %grad_ref.1), custom_call_target="tpu_custom_call" | custom-call | flops 268435456 | bytes 4194304 | tf_op jit(solution)/shard_map/tiles_here/pallas_call | solution.py:232
  8.9 0.0 collective-permute-done.16.refs_1_
  9.0 0.0 copy-start
  9.0 0.5 copy-done
  9.5 1.8 %plan.1 = (s32[1]{0:T(128)}, s32[16]{0:T(128)S(1)}, s32[16]{0:T(128)S(1)}) custom-call(s32[33]{0:T(128)S(1)} %pad_add_fusion.refs_0_.list_ref.place_ref, s32[33]{0:T(128)} %copy-done), custom_call_target="tpu_custom_call" | custom-call | tf_op jit(solution)/shard_map/plan/pallas_call | solution.py:70
  11.9 44.3 %conditional.1 = ((f32[8,128,128]{2,1,0:T(8,128)S(1)}, f32[8,128,128]{2,1,0:T(8,128)S(1)})) conditional(s32[]{:T(128)} %bitcast, (f32[8,128,128]{2,1,0:T(8,128)S(1)}, f32[8,128,128]{2,1,0:T(8,128)S(1)}) %tiles_here.1, (s32[16]{0:T(128)S(1)}, bf16[1024,2048]{1,0:T(8,128)(2,1)}, s32[33]{0:T(128)S(1)}, s32[16]{0:T(128)S(1)}, ...), branch_computations={%region_0.0_spmd, %region_1.0_spmd, %region_2.0_spmd, %region_3.0_... | conditional | flops 268435456 | bytes 29360176 | solution.py:276
  12.0 3.2 %pack.21 = bf16[6,1024,128]{2,1,0:T(8,128)(2,1)} custom-call(s32[16]{0:T(128)S(1)} %get-tuple-element.270.send_ref, bf16[1024,2048]{1,0:T(8,128)(2,1)} %get-tuple-element.271.act_ref), custom_call_target="tpu_custom_call" | custom-call | bytes 3145728 | tf_op jit(solution)/shard_map/cond/branch_6_fun/pack/pallas_call | solution.py:101
  15.1 1.7 %collective-permute-start.5 = (bf16[6,1024,128]{2,1,0:T(8,128)(2,1)}, bf16[6,1024,128]{2,1,0:T(8,128)(2,1)S(1)}, u32[]{:S(2)}, u32[]{:S(2)}) collective-permute-start(bf16[6,1024,128]{2,1,0:T(8,128)(2,1)} %pack.21), channel_id=1, source_target_pairs={{0,1},{1,0},{2,3},{3,2},{4,5},{5,4},{6,7},{7,6},{8,9},{9,8},{10,11... | collective-permute-start | bytes 4718600 | tf_op jit(solution)/shard_map/cond/branch_6_fun/ppermute | solution.py:272
  16.9 34.7 %collective-permute-done.5.rows_ref = bf16[6,1024,128]{2,1,0:T(8,128)(2,1)S(1)} collective-permute-done((bf16[6,1024,128]{2,1,0:T(8,128)(2,1)}, bf16[6,1024,128]{2,1,0:T(8,128)(2,1)S(1)}, u32[]{:S(2)}, u32[]{:S(2)}) %collective-permute-start.5) | collective-permute-done | bytes 1572896 | tf_op jit(solution)/shard_map/cond/branch_6_fun/ppermute | solution.py:272
  51.6 4.6 %tiles_moved.21 = (f32[8,128,128]{2,1,0:T(8,128)S(1)}, f32[8,128,128]{2,1,0:T(8,128)S(1)}) custom-call(s32[33]{0:T(128)S(1)} %get-tuple-element.268.list_ref, s32[16]{0:T(128)S(1)} %get-tuple-element.269.place_ref, bf16[6,1024,128]{2,1,0:T(8,128)(2,1)S(1)} %collective-permute-done.5.rows_ref, ...), custom_call_target="tpu_custom_call", output_to_operand_aliasing={{0}: (4, {}), {1}: (5, {})} | custom-call | flops 268435456 | bytes 4194304 | tf_op jit(solution)/shard_map/cond/branch_6_fun/tiles_moved/pallas_call | solution.py:232
  56.2 0.1 collective-permute-start.17
  56.3 1.9 %collective-permute-done.17 = f32[8,128,128]{2,1,0:T(8,128)S(1)} collective-permute-done((f32[8,128,128]{2,1,0:T(8,128)S(1)}, f32[8,128,128]{2,1,0:T(8,128)S(1)}, u32[]{:S(2)}, u32[]{:S(2)}) %collective-permute-start.17) | collective-permute-done | bytes 524320 | tf_op jit(solution)/shard_map/ppermute | solution.py:283
  58.2 0.1 slice_add_fusion.1
  58.3 1.8 %collective-permute-start.18 = (f32[4,128,128]{2,1,0:T(8,128)S(1)}, f32[4,128,128]{2,1,0:T(8,128)S(1)}, u32[]{:S(2)}, u32[]{:S(2)}) collective-permute-start(f32[4,128,128]{2,1,0:T(8,128)S(1)} %get-tuple-element.360), channel_id=1, source_target_pairs={{0,4},{2,6},{4,0},{6,2},{8,12},{10,14},{12,8},{14,10},{16,20},{18,... | collective-permute-start | bytes 786440 | tf_op jit(solution)/shard_map/ppermute | solution.py:283
  60.1 6.6 %collective-permute-done.18 = f32[4,128,128]{2,1,0:T(8,128)S(1)} collective-permute-done((f32[4,128,128]{2,1,0:T(8,128)S(1)}, f32[4,128,128]{2,1,0:T(8,128)S(1)}, u32[]{:S(2)}, u32[]{:S(2)}) %collective-permute-start.18) | collective-permute-done | bytes 262176 | tf_op jit(solution)/shard_map/ppermute | solution.py:283
  66.7 1.9 %collective-permute-start.19 = (f32[2,128,128]{2,1,0:T(8,128)S(1)}, f32[2,128,128]{2,1,0:T(8,128)S(1)}, u32[]{:S(2)}, u32[]{:S(2)}) collective-permute-start(f32[2,128,128]{2,1,0:T(8,128)S(1)} %get-tuple-element.362), channel_id=1, source_target_pairs={{0,8},{2,10},{4,12},{6,14},{8,0},{10,2},{12,4},{14,6},{16,24},{18,... | collective-permute-start | bytes 393224 | tf_op jit(solution)/shard_map/ppermute | solution.py:283
  68.6 3.2 %collective-permute-done.19 = f32[2,128,128]{2,1,0:T(8,128)S(1)} collective-permute-done((f32[2,128,128]{2,1,0:T(8,128)S(1)}, f32[2,128,128]{2,1,0:T(8,128)S(1)}, u32[]{:S(2)}, u32[]{:S(2)}) %collective-permute-start.19) | collective-permute-done | bytes 131104 | tf_op jit(solution)/shard_map/ppermute | solution.py:283
  71.8 2.8 %collective-permute-start.20 = (f32[1,128,128]{2,1,0:T(8,128)S(1)}, f32[1,128,128]{2,1,0:T(8,128)S(1)}, u32[]{:S(2)}, u32[]{:S(2)}) collective-permute-start(f32[1,128,128]{2,1,0:T(8,128)S(1)} %slice_add_fusion.4), channel_id=1, source_target_pairs={{0,16},{2,18},{4,20},{6,22},{8,24},{10,26},{12,28},{14,30},{16,0},... | collective-permute-start | bytes 196616 | tf_op jit(solution)/shard_map/ppermute | solution.py:283
  74.6 2.5 %collective-permute-done.20 = f32[1,128,128]{2,1,0:T(8,128)S(1)} collective-permute-done((f32[1,128,128]{2,1,0:T(8,128)S(1)}, f32[1,128,128]{2,1,0:T(8,128)S(1)}, u32[]{:S(2)}, u32[]{:S(2)}) %collective-permute-start.20) | collective-permute-done | bytes 65568 | tf_op jit(solution)/shard_map/ppermute | solution.py:283
  77.0 0.6 fusion.1
  (2 shorter events, 0.0 us)
Async XLA Ops:
  1.6 7.4 %collective-permute-start.16 = (s32[33]{0:T(128)S(1)}, s32[33]{0:T(128)S(1)}, u32[]{:S(2)}, u32[]{:S(2)}) collective-permute-start(s32[33]{0:T(128)S(1)} %pad_add_fusion.refs_0_.list_ref.place_ref), channel_id=1, source_target_pairs={{0,1},{1,0},{2,3},{3,2},{4,5},{5,4},{6,7},{7,6},{8,9},{9,8},{10,11... | collective-permute-start | bytes 404 | tf_op jit(solution)/shard_map/ppermute | solution.py:262
  9.0 0.5 copy-start
  15.1 36.5 %collective-permute-start.5 = (bf16[6,1024,128]{2,1,0:T(8,128)(2,1)}, bf16[6,1024,128]{2,1,0:T(8,128)(2,1)S(1)}, u32[]{:S(2)}, u32[]{:S(2)}) collective-permute-start(bf16[6,1024,128]{2,1,0:T(8,128)(2,1)} %pack.21), channel_id=1, source_target_pairs={{0,1},{1,0},{2,3},{3,2},{4,5},{5,4},{6,7},{7,6},{8,9},{9,8},{10,11... | collective-permute-start | bytes 4718600 | tf_op jit(solution)/shard_map/cond/branch_6_fun/ppermute | solution.py:272
  56.2 2.0 %collective-permute-start.17 = (f32[8,128,128]{2,1,0:T(8,128)S(1)}, f32[8,128,128]{2,1,0:T(8,128)S(1)}, u32[]{:S(2)}, u32[]{:S(2)}) collective-permute-start(f32[8,128,128]{2,1,0:T(8,128)S(1)} %get-tuple-element.358), channel_id=1, source_target_pairs={{0,2},{2,0},{4,6},{6,4},{8,10},{10,8},{12,14},{14,12},{16,18},{18,... | collective-permute-start | bytes 1572872 | tf_op jit(solution)/shard_map/ppermute | solution.py:283
  58.3 8.4 %collective-permute-start.18 = (f32[4,128,128]{2,1,0:T(8,128)S(1)}, f32[4,128,128]{2,1,0:T(8,128)S(1)}, u32[]{:S(2)}, u32[]{:S(2)}) collective-permute-start(f32[4,128,128]{2,1,0:T(8,128)S(1)} %get-tuple-element.360), channel_id=1, source_target_pairs={{0,4},{2,6},{4,0},{6,2},{8,12},{10,14},{12,8},{14,10},{16,20},{18,... | collective-permute-start | bytes 786440 | tf_op jit(solution)/shard_map/ppermute | solution.py:283
  66.7 5.0 %collective-permute-start.19 = (f32[2,128,128]{2,1,0:T(8,128)S(1)}, f32[2,128,128]{2,1,0:T(8,128)S(1)}, u32[]{:S(2)}, u32[]{:S(2)}) collective-permute-start(f32[2,128,128]{2,1,0:T(8,128)S(1)} %get-tuple-element.362), channel_id=1, source_target_pairs={{0,8},{2,10},{4,12},{6,14},{8,0},{10,2},{12,4},{14,6},{16,24},{18,... | collective-permute-start | bytes 393224 | tf_op jit(solution)/shard_map/ppermute | solution.py:283
  71.8 5.2 %collective-permute-start.20 = (f32[1,128,128]{2,1,0:T(8,128)S(1)}, f32[1,128,128]{2,1,0:T(8,128)S(1)}, u32[]{:S(2)}, u32[]{:S(2)}) collective-permute-start(f32[1,128,128]{2,1,0:T(8,128)S(1)} %slice_add_fusion.4), channel_id=1, source_target_pairs={{0,16},{2,18},{4,20},{6,22},{8,24},{10,26},{12,28},{14,30},{16,0},... | collective-permute-start | bytes 196616 | tf_op jit(solution)/shard_map/ppermute | solution.py:283
